TPU v7x, 32 devices: a whole 2x2x4 slice. The times are simulated.
32 devices in a mesh: batch: 4 (over x, core), gene: 8 (over z, y).
Axes of the slice: x: 2, y: 2, z: 4, core: 2. Of those that a mesh axis runs over, the one named last changes fastest.
Arguments:
- counts_in: float32 [7168, 8192], P('gene', 'batch'), may hold values from 0 to 6
- umi_total: int32 [8192], P('batch'), may hold values from 2500 to 39999
- gene_mask: int32 [7168], P('gene'), may hold values 0 or 1
- noise: float32 [100, 8192], P(None, 'batch'), may hold values from -6 to 6
- w_enc: float32 [7168, 800], P('gene'), may hold values from -0.0625 to 0.0625
- gain_enc: float32 [800], P('gene'), may hold values from 0.25 to 1.75
- shift_enc: float32 [800], P('gene'), may hold values from -3 to 3
- w_lat: float32 [200, 800], replicated, may hold values from -0.21875 to 0.21875
- b_lat: float32 [200], replicated, may hold values from -2 to 2
- w_dec: float32 [100, 800], replicated, may hold values from -0.625 to 0.625
- gain_dec: float32 [800], replicated, may hold values from 0.25 to 1.75
- shift_dec: float32 [800], replicated, may hold values from -3 to 3
- w_out: float32 [7168, 800], P('gene'), may hold values from -0.21875 to 0.21875
- b_out: float32 [7168], P('gene'), may hold values from -3 to 3
- mean_enc: float32 [800], P('gene'), may hold values from -3 to 3
- var_enc: float32 [800], P('gene'), may hold values from 0.5 to 2
- mean_dec: float32 [800], replicated, may hold values from -3 to 3
- var_dec: float32 [800], replicated, may hold values from 0.5 to 2
Outputs:
- recon: float32 [7168, 8192], P('gene', 'batch')
- grad_counts: float32 [7168, 8192], P('gene', 'batch')
- grad_w_enc: float32 [7168, 800], P('gene')
- grad_gain_enc: float32 [800], P('gene')
- grad_shift_enc: float32 [800], P('gene')
- grad_w_lat: float32 [200, 800], P(None, 'gene')
- grad_b_lat: float32 [200], replicated
- grad_w_dec: float32 [100, 800], P(None, 'gene')
- grad_gain_dec: float32 [800], P('gene')
- grad_shift_dec: float32 [800], P('gene')
- grad_w_out: float32 [7168, 800], P('gene')
- grad_b_out: float32 [7168], P('gene')
- new_mean_enc: float32 [800], P('gene')
- new_var_enc: float32 [800], P('gene')
- new_mean_dec: float32 [800], replicated
- new_var_dec: float32 [800], replicated
All inputs are finite; a program needn't handle non-finite values. No bound on the sum of `gene_mask` on one device may be relied on, other than what follows from the above.
Results may differ from a plain program's by a relative error of at most 0.00023.
Values sent between devices are 32-bit elements; how exact they have to be, the bound alone decides.
No kernel may reach another device: no remote copies, remote signals or barrier semaphores. Data moves between devices by JAX's collectives and lax.ppermute only.
A program may use at most 128 MiB of HBM per device.

v0:
```python
import jax
import jax.numpy as jnp
from jax import lax
from jax.sharding import PartitionSpec as P

ALPHA = 0.002
BN_EPS = 1e-05
MOMENTUM = 0.1
UMI_SCALE = 10000.0


def contract(left, right, left_dim, right_dim):
    return lax.dot_general(
        left,
        right,
        (((left_dim,), (right_dim,)), ((), ())),
        precision=lax.Precision.HIGHEST,
        preferred_element_type=jnp.float32,
    )


def silu_slope(value):
    sig = jax.nn.sigmoid(value)
    return sig * (1.0 + value * (1.0 - sig))


def on_device(
    counts_in,
    umi_total,
    gene_mask,
    noise,
    w_enc,
    gain_enc,
    shift_enc,
    w_lat,
    b_lat,
    w_dec,
    gain_dec,
    shift_dec,
    w_out,
    b_out,
    mean_enc,
    var_enc,
    mean_dec,
    var_dec,
):
    cells = counts_in.shape[1] * lax.axis_size("batch")
    hidden = w_enc.shape[1]
    share = hidden // lax.axis_size("gene")
    latent = noise.shape[0]
    offset = lax.axis_index("gene") * share
    factor = UMI_SCALE / umi_total.astype(jnp.float32)
    maskf = gene_mask.astype(jnp.float32)
    scaled = counts_in * factor[None, :] * maskf[:, None]
    pre_enc = lax.psum_scatter(
        contract(w_enc, scaled, 0, 0), "gene", scatter_dimension=0, tiled=True
    )
    mean1 = lax.psum(jnp.sum(pre_enc, axis=1), "batch") / cells
    cent1 = pre_enc - mean1[:, None]
    var1 = lax.psum(jnp.sum(cent1 * cent1, axis=1), "batch") / cells
    rstd1 = lax.rsqrt(var1 + BN_EPS)
    norm1 = cent1 * rstd1[:, None]
    in1 = norm1 * gain_enc[:, None] + shift_enc[:, None]
    act1 = jax.nn.silu(in1)
    lat_cols = lax.dynamic_slice_in_dim(w_lat, offset, share, 1)
    act_full = lax.all_gather(act1, "gene", axis=0, tiled=True)
    lat = contract(w_lat, act_full, 1, 0)
    lat = lat + b_lat[:, None]
    mu = lat[:latent]
    logvar = lat[latent:]
    spread = jnp.exp(0.5 * logvar)
    z = mu + spread * noise
    pre_dec = contract(w_dec, z, 0, 0)
    mean2 = lax.psum(jnp.sum(pre_dec, axis=1), "batch") / cells
    cent2 = pre_dec - mean2[:, None]
    var2 = lax.psum(jnp.sum(cent2 * cent2, axis=1), "batch") / cells
    rstd2 = lax.rsqrt(var2 + BN_EPS)
    norm2 = cent2 * rstd2[:, None]
    in2 = norm2 * gain_dec[:, None] + shift_dec[:, None]
    act2 = jax.nn.silu(in2)
    pre_out = contract(w_out, act2, 1, 0) + b_out[:, None]
    recon = jax.nn.softplus(pre_out)
    diff = maskf[:, None] * (recon - scaled) / cells
    grad_pre = diff * jax.nn.sigmoid(pre_out)
    grad_w_out = contract(grad_pre, act2, 1, 1)
    grad_b_out = jnp.sum(grad_pre, axis=1)
    grad_act2 = lax.psum_scatter(
        contract(w_out, grad_pre, 0, 0), "gene", scatter_dimension=0, tiled=True
    )
    norm2_part = lax.dynamic_slice_in_dim(norm2, offset, share, 0)
    in2_part = lax.dynamic_slice_in_dim(in2, offset, share, 0)
    grad_in2 = grad_act2 * silu_slope(in2_part)
    grad_shift_dec, grad_gain_dec = lax.psum(
        (jnp.sum(grad_in2, axis=1), jnp.sum(grad_in2 * norm2_part, axis=1)), "batch"
    )
    scale2 = lax.dynamic_slice_in_dim(gain_dec * rstd2, offset, share, 0)
    grad_pre_dec = scale2[:, None] * (
        grad_in2 - grad_shift_dec[:, None] / cells - norm2_part * grad_gain_dec[:, None] / cells
    )
    dec_cols = lax.dynamic_slice_in_dim(w_dec, offset, share, 1)
    grad_w_dec = contract(z, grad_pre_dec, 1, 1)
    grad_z = lax.psum(contract(dec_cols, grad_pre_dec, 1, 0), "gene")
    grad_mu = grad_z + ALPHA * mu / cells
    grad_logvar = 0.5 * grad_z * noise * spread + 0.5 * ALPHA * (jnp.exp(logvar) - 1.0) / cells
    grad_lat = jnp.concatenate([grad_mu, grad_logvar], axis=0)
    grad_w_lat = contract(grad_lat, act1, 1, 1)
    grad_b_lat = jnp.sum(grad_lat, axis=1)
    grad_act1 = contract(lat_cols, grad_lat, 0, 0)
    grad_in1 = grad_act1 * silu_slope(in1)
    grad_shift_enc, grad_gain_enc = lax.psum(
        (jnp.sum(grad_in1, axis=1), jnp.sum(grad_in1 * norm1, axis=1)), "batch"
    )
    grad_pre_enc = (gain_enc * rstd1)[:, None] * (
        grad_in1 - grad_shift_enc[:, None] / cells - norm1 * grad_gain_enc[:, None] / cells
    )
    piece = lax.all_gather(grad_pre_enc, "gene", axis=0, tiled=True)
    grad_scaled = -diff
    grad_scaled = grad_scaled + contract(w_enc, piece, 1, 0)
    grad_weight = contract(scaled, piece, 1, 1)
    grad_scaled, grad_w_enc = (grad_scaled, grad_weight)
    grad_counts = grad_scaled * factor[None, :] * maskf[:, None]
    grad_w_enc, grad_w_out, grad_b_out, grad_w_dec, grad_w_lat, grad_b_lat = lax.psum(
        (grad_w_enc, grad_w_out, grad_b_out, grad_w_dec, grad_w_lat, grad_b_lat), "batch"
    )
    correct = cells / (cells - 1.0)
    new_mean_enc = (1.0 - MOMENTUM) * mean_enc + MOMENTUM * mean1
    new_var_enc = (1.0 - MOMENTUM) * var_enc + MOMENTUM * var1 * correct
    new_mean_dec = (1.0 - MOMENTUM) * mean_dec + MOMENTUM * mean2
    new_var_dec = (1.0 - MOMENTUM) * var_dec + MOMENTUM * var2 * correct
    return (
        recon,
        grad_counts,
        grad_w_enc,
        grad_gain_enc,
        grad_shift_enc,
        grad_w_lat,
        grad_b_lat,
        grad_w_dec,
        grad_gain_dec,
        grad_shift_dec,
        grad_w_out,
        grad_b_out,
        new_mean_enc,
        new_var_enc,
        new_mean_dec,
        new_var_dec,
    )


def solution(mesh):
    return jax.shard_map(
        on_device,
        mesh=mesh,
        in_specs=(
            P("gene", "batch"),
            P("batch"),
            P("gene"),
            P(None, "batch"),
            P("gene", None),
            P("gene"),
            P("gene"),
            P(),
            P(),
            P(),
            P(),
            P(),
            P("gene", None),
            P("gene"),
            P("gene"),
            P("gene"),
            P(),
            P(),
        ),
        out_specs=(
            P("gene", "batch"),
            P("gene", "batch"),
            P("gene", None),
            P("gene"),
            P("gene"),
            P(None, "gene"),
            P(),
            P(None, "gene"),
            P("gene"),
            P("gene"),
            P("gene", None),
            P("gene"),
            P("gene"),
            P("gene"),
            P(),
            P(),
        ),
        check_vma=False,
    )
```

profile of v0, /device:TPU:0, one launch (start us, length us, event | category | flops | bytes accessed | tf_op | source)
XLA Modules:
  0.0 952.4 jit_solution(2008415696607780730)
XLA Ops:
  7.3 8.7 copy.40
  16.0 26.0 %fusion.17 = f32[800,2048]{1,0:T(8,128)} fusion(f32[896,800]{0,1:T(8,128)} %param.22, f32[896,2048]{0,1:T(8,128)} %copy.40, f32[896]{0:T(1024)S(1)} %convert_element_type.7, f32[2048]{0:T(1024)S(1)} %convert_divide_fusion), kind=kOutput, calls=%fused_computation.28 | convolution fusion | flops 17619746816 | bytes 16772608 | tf_op jit(solution)/shard_map/dot_general | solution.py:13
  42.0 142.4 %fusion = f32[104,2048]{1,0:T(8,128)} fusion(f32[800,2048]{1,0:T(8,128)} %fusion.17), kind=kCustom, calls=%all-reduce-scatter | all-reduce-scatter fusion | flops 1703937 | bytes 7406080
  205.3 6.6 psum.106
  215.8 108.2 %all-gather.5.cloned.1.call-done = f32[8,100,2048]{2,1,0:T(8,128)} async-done(((f32[1,100,2048]{2,1,0:T(8,128)}), f32[8,100,2048]{2,1,0:T(8,128)}) %all-gather.5.cloned.1.call-update) | async-done | bytes 6553616 | tf_op jit(solution)/shard_map/all_gather | solution.py:66
  323.9 6.2 reshape.53
  330.1 8.4 fusion.22
  338.6 7.4 fusion.58
  346.0 6.2 psum.107
  356.4 6.3 psum.108
  368.8 38.7 %fusion.56 = (f32[896]{0:T(1024)S(1)}, f32[896,2048]{0,1:T(8,128)S(1)}, f32[896,2048]{0,1:T(8,128)}, f32[2048,896]{1,0:T(8,128)}) fusion(f32[896,2048]{0,1:T(8,128)} %copy.40, f32[2048]{0:T(1024)S(1)} %convert_divide_fusion, f32[896]{0:T(1024)S(1)} %copy-done.28, f32[896]{0:T(1024)S(1)} %convert_element_type.7, f32[896,800]{0,1:T(8,128)S(1)} %copy-done, ...), kind=kOutput, calls=%fused_computation.94 | convolution fusion | flops 17653825536 | bytes 38799872 | tf_op jit(solution)/shard_map/dot_general | solution.py:13
  410.6 23.1 %convolution_bitcast_fusion = f32[800,2048]{1,0:T(8,128)} fusion(f32[896,2048]{0,1:T(8,128)S(1)} %get-tuple-element.79, f32[896,800]{0,1:T(8,128)S(1)} %copy-done), kind=kOutput, calls=%fused_computation.27 | convolution fusion | flops 17616076800 | bytes 16760832 | tf_op jit(solution)/shard_map/dot_general | solution.py:13
  433.7 134.8 %fusion.1 = f32[104,2048]{1,0:T(8,128)S(1)} fusion(f32[800,2048]{1,0:T(8,128)} %convolution_bitcast_fusion), kind=kCustom, calls=%all-reduce-scatter.1 | all-reduce-scatter fusion | flops 1703937 | bytes 7406080
  582.5 5.8 all-reduce.5
  594.9 76.9 %all-reduce.10.cloned.1.call-done = f32[100,2048]{1,0:T(8,128)} async-done(((f32[100,2048]{1,0:T(8,128)}), f32[100,2048]{1,0:T(8,128)}) %all-reduce.10.cloned.1.call-update) | async-done | bytes 819216 | tf_op jit(solution)/shard_map/psum | solution.py:102
  676.8 11.3 %all-reduce.4 = (f32[100]{0:T(128)S(1)}, f32[100]{0:T(128)S(1)}, f32[200]{0:T(256)}, f32[100,100]{1,0:T(8,128)}, f32[896]{0:T(1024)}) all-reduce(f32[100]{0:T(128)S(1)} %get-tuple-element.65, f32[100]{0:T(128)S(1)} %get-tuple-element.64, f32[200]{0:T(256)S(1)} %fusion.25, ...), channel_id=1, replica_groups=mesh['batch'=4,'gene'=8] {'batch'}, use_global_device_ids=true, to_apply=%region_18.19 | all-reduce | flops 11296 | bytes 90368 | tf_op jit(solution)/shard_map/psum | solution.py:110
  689.5 25.9 %fusion.23 = f32[896,800]{0,1:T(8,128)} fusion(f32[896,2048]{0,1:T(8,128)} %copy-done.31, f32[2048,800]{0,1:T(8,128)} %copy-done.5), kind=kOutput, calls=%fused_computation.37 | convolution fusion | flops 17622630400 | bytes 16760832 | tf_op jit(solution)/shard_map/dot_general | solution.py:13
  717.8 76.9 %all-gather.7.cloned.1.call-done = f32[8,100,2048]{2,1,0:T(8,128)} async-done(((f32[1,100,2048]{2,1,0:T(8,128)}), f32[8,100,2048]{2,1,0:T(8,128)}) %all-gather.7.cloned.1.call-update) | async-done | bytes 6553616 | tf_op jit(solution)/shard_map/all_gather | solution.py:116
  794.8 6.2 reshape.55
  801.0 26.7 %fusion.15 = f32[896,800]{0,1:T(8,128)} fusion(f32[800,2048]{1,0:T(8,128)} %reshape.55, f32[896,2048]{0,1:T(8,128)} %copy.40, f32[896]{0:T(1024)S(1)} %convert_element_type.7, f32[2048]{0:T(1024)S(1)} %convert_divide_fusion), kind=kOutput, calls=%fused_computation.25 | convolution fusion | flops 17619746816 | bytes 16772608 | tf_op jit(solution)/shard_map/dot_general | solution.py:13
  827.6 8.6 copy.41
  836.2 35.8 %fusion.3 = f32[896,2048]{0,1:T(8,128)} fusion(f32[800,2048]{1,0:T(8,128)} %reshape.55, f32[896,800]{0,1:T(8,128)S(1)} %copy-done.27, f32[896]{0:T(1024)S(1)} %convert_element_type.7, f32[2048]{0:T(1024)S(1)} %convert_divide_fusion, f32[896,2048]{0,1:T(8,128)} %copy.40, f32[2048,896]{1,0:T(8,128)} %get-tuple-element.98, f32[896]{0:T(1024)S(1)} %copy-done.28), kind=kOutput, calls=%fused_computation.3 | convolution fusion | flops 17645436928 | bytes 31456256 | tf_op jit(solution)/shard_map/dot_general | solution.py:13
  872.0 8.7 copy.42
  880.7 58.2 %all-reduce.12.cloned.1.call-done = (f32[896,800]{0,1:T(8,128)}, f32[200,100]{1,0:T(8,128)}, f32[896,800]{0,1:T(8,128)}) async-done(((f32[896,800]{0,1:T(8,128)}, f32[200,100]{1,0:T(8,128)}, f32[896,800]{0,1:T(8,128)}), (f32[896,800]{0,1:T(8,128)}, f32[200,100]{1,0:T(8,128)}, f32[896,800]{0,1:T(8,128)})) %all-reduce.12.cloned.1.call-update) | async-done | bytes 5814416 | tf_op jit(solution)/shard_map/psum | solution.py:122
  (107 shorter events, 73.5 us)
Async XLA Ops:
  7.2 361.6 %copy-start = (f32[896,800]{0,1:T(8,128)S(1)}, f32[896,800]{0,1:T(8,128)}, u32[]{:S(2)}) copy-start(f32[896,800]{0,1:T(8,128)} %param.30) | copy-start | bytes 8601604
  7.2 316.7 %all-gather.5.cloned.1.call-start = ((), (), s32[]{:S(2)}) async-start(), calls=%async_computation.1 | async-start | bytes 7667712 | tf_op jit(solution)/shard_map/all_gather | solution.py:66
  42.0 144.8 %copy-start.24 = (u32[32]{0:T(128)S(1)}, u32[32]{0:T(128)}, u32[]{:S(2)}) copy-start(u32[32]{0:T(128)} %constant.74) | copy-start | bytes 388
  42.0 161.3 %copy-start.25 = (f32[100]{0:T(128)S(1)}, f32[100]{0:T(128)}, u32[]{:S(2)}) copy-start(f32[100]{0:T(128)} %param.32) | copy-start | bytes 1204
  42.0 169.9 %copy-start.20 = (f32[100]{0:T(128)S(1)}, f32[100]{0:T(128)}, u32[]{:S(2)}) copy-start(f32[100]{0:T(128)} %param.23) | copy-start | bytes 1204
  42.0 169.9 %copy-start.26 = (f32[100]{0:T(128)S(1)}, f32[100]{0:T(128)}, u32[]{:S(2)}) copy-start(f32[100]{0:T(128)} %param.33) | copy-start | bytes 1204
  42.0 170.4 %copy-start.21 = (f32[100]{0:T(128)S(1)}, f32[100]{0:T(128)}, u32[]{:S(2)}) copy-start(f32[100]{0:T(128)} %param.24) | copy-start | bytes 1204
  185.4 6.8 collective-permute-start
  215.2 114.9 %copy-start.15 = (f32[200]{0:T(256)S(1)}, f32[200]{0:T(256)}, u32[]{:S(2)}) copy-start(f32[200]{0:T(256)} %param.26) | copy-start | bytes 2404
  215.2 456.6 %all-reduce.10.cloned.1.call-start = ((), (), s32[]{:S(2)}) async-start(), calls=%async_computation | async-start | bytes 1703936 | tf_op jit(solution)/shard_map/psum | solution.py:102
  346.0 17.3 %copy-start.19 = (f32[800]{0:T(1024)S(1)}, f32[800]{0:T(1024)}, u32[]{:S(2)}) copy-start(f32[800]{0:T(1024)} %param.29) | copy-start | bytes 9604
  368.8 38.7 %copy-start.5 = (f32[2048,800]{0,1:T(8,128)}, f32[2048,800]{0,1:T(8,128)S(1)}, u32[]{:S(2)}) copy-start(f32[2048,800]{0,1:T(8,128)S(1)} %get-tuple-element.81) | copy-start | bytes 19660804
  568.5 23.4 %copy-start.3 = (f32[200,2048]{1,0:T(8,128)S(1)}, f32[200,2048]{1,0:T(8,128)}, u32[]{:S(2)}) copy-start(f32[200,2048]{1,0:T(8,128)} %copy-done.2) | copy-start | bytes 4915204
  568.6 6.8 collective-permute-start.1
  582.5 91.2 %copy-start.4 = (f32[132,2048]{1,0:T(8,128)S(1)}, f32[132,2048]{1,0:T(8,128)}, u32[]{:S(2)}) copy-start(f32[132,2048]{1,0:T(8,128)} %concatenate.4) | copy-start | bytes 3244036
  588.3 88.2 %copy-start.22 = (f32[100]{0:T(128)}, f32[100]{0:T(128)S(1)}, u32[]{:S(2)}) copy-start(f32[100]{0:T(128)S(1)} %get-tuple-element.108) | copy-start | bytes 1204
  588.3 88.2 %copy-start.30 = (f32[100]{0:T(128)}, f32[100]{0:T(128)S(1)}, u32[]{:S(2)}) copy-start(f32[100]{0:T(128)S(1)} %get-tuple-element.109) | copy-start | bytes 1204
  591.9 202.9 %all-gather.7.cloned.1.call-start = ((), (), s32[]{:S(2)}) async-start(), calls=%async_computation.2 | async-start | bytes 7667712 | tf_op jit(solution)/shard_map/all_gather | solution.py:116
  688.1 27.3 %copy-start.23 = (f32[100]{0:T(128)}, f32[100]{0:T(128)S(1)}, u32[]{:S(2)}) copy-start(f32[100]{0:T(128)S(1)} %get-tuple-element.103) | copy-start | bytes 1204
  688.1 27.3 %copy-start.29 = (f32[100]{0:T(128)}, f32[100]{0:T(128)S(1)}, u32[]{:S(2)}) copy-start(f32[100]{0:T(128)S(1)} %get-tuple-element.104) | copy-start | bytes 1204
  689.4 26.0 %copy-start.8 = (f32[100,2048]{1,0:T(8,128)S(1)}, f32[100,2048]{1,0:T(8,128)}, u32[]{:S(2)}) copy-start(f32[100,2048]{1,0:T(8,128)} %copy-done.7) | copy-start | bytes 2457604
  689.4 26.0 %copy-start.10 = (f32[100,2048]{1,0:T(8,128)S(1)}, f32[100,2048]{1,0:T(8,128)}, u32[]{:S(2)}) copy-start(f32[100,2048]{1,0:T(8,128)} %copy-done.9) | copy-start | bytes 2457604
  689.4 249.4 %all-reduce.12.cloned.1.call-start = ((), (), s32[]{:S(2)}) async-start(), calls=%async_computation.3 | async-start | bytes 11673600 | tf_op jit(solution)/shard_map/psum | solution.py:122
  872.0 73.7 %copy-start.1 = (f32[896,800]{0,1:T(8,128)S(1)}, f32[896,800]{0,1:T(8,128)}, u32[]{:S(2)}) copy-start(f32[896,800]{0,1:T(8,128)} %param.30) | copy-start | bytes 8601604
  (14 other events, 117.2 us)
Sparse Core Ops, SparseCore 0:
  215.3 108.5 all-gather.4
  592.0 79.7 all-reduce.9
  689.5 105.2 all-gather.6
  827.8 111.0 all-reduce.11
where the time goes:
time: 962 us; the launch traced here: 952 us
  waiting for transfers between devices  329 us (34%)
  blocking collectives  319 us (33%)
  matrix products  204 us (21%)
  local copies, waits for them, and re-layouts  58 us (6%)
  other arithmetic  23.5 us (2%)
  between operations  15 us (2%)
    unnamed x2, blocking collectives  277 us
    dot_general x12, matrix products, contract(): lax.dot_general(left, right, (((left_dim,), (right_dim,)), ((), ())), pre...  204 us
    all_gather x1, waiting for transfers between devices, on_device(): act_full = lax.all_gather(act1, 'gene', axis=0, tiled=True)  108 us
    psum x1, waiting for transfers between devices, on_device(): grad_z = lax.psum(contract(dec_cols, grad_pre_dec, 1, 0), 'gene')  76.9 us
    all_gather x1, waiting for transfers between devices, on_device(): piece = lax.all_gather(grad_pre_enc, 'gene', axis=0, tiled=True)  76.9 us
    psum x1, waiting for transfers between devices, on_device(): lax.psum((grad_w_enc, grad_w_out, grad_b_out, grad_w_dec, grad_w_lat, gra...  58.2 us
    unnamed x77, local copies, waits for them, and re-layouts  58 us
  transfers between devices with their start and end apart: 6, of which 6 were waited for; matrix products, arithmetic and copies ran while one was open for 9% of the time, Pallas kernels for 0%

commit v1 on v0

v1 whole, which is shorter than its diff:
```python
import jax
import jax.numpy as jnp
from jax import lax
from jax.experimental import pallas as pl
from jax.experimental.pallas import tpu as pltpu
from jax.sharding import PartitionSpec as P

ALPHA = 0.002
BN_EPS = 1e-05
MOMENTUM = 0.1
UMI_SCALE = 10000.0
BATCH = "batch"
GENE = "gene"
TILE = 256
VMEM_BYTES = 56 << 20
F32 = jnp.float32


BF16 = jnp.bfloat16
RATE = 1_100_000_000


def split(value):
    high = value.astype(BF16)
    return high, (value - high.astype(F32)).astype(BF16)


def whole(pair):
    return pair[0].astype(F32) + pair[1].astype(F32)


def dot(left, right, left_dim, right_dim):
    def one(a, b):
        return lax.dot_general(
            a,
            b,
            (((left_dim,), (right_dim,)), ((), ())),
            preferred_element_type=F32,
        )

    return one(left[0], right[0]) + (one(left[0], right[1]) + one(left[1], right[0]))


def kernel_call(
    body, grid, in_specs, out_specs, out_shape, micros, order=None, scratch=(), after=()
):
    leading = 0 if order is None else 1
    held = leading + len(in_specs)

    def run(*refs):
        body(*refs[:held], *refs[held + len(after) :])

    call = pl.pallas_call(
        run,
        grid_spec=pltpu.PrefetchScalarGridSpec(
            num_scalar_prefetch=leading,
            grid=grid,
            in_specs=list(in_specs) + [pl.BlockSpec(memory_space=pl.ANY)] * len(after),
            out_specs=out_specs,
            scratch_shapes=list(scratch),
        ),
        out_shape=out_shape,
        compiler_params=pltpu.CompilerParams(vmem_limit_bytes=VMEM_BYTES),
        cost_estimate=pl.CostEstimate(
            flops=int(micros * RATE), bytes_accessed=1024, transcendentals=0
        ),
    )
    prefetch = () if order is None else (order,)
    return lambda *args: call(*prefetch, *args, *after)


def shape(*dims, dtype=F32):
    return jax.ShapeDtypeStruct(dims, dtype)


def full(*dims):
    return pl.BlockSpec(dims, lambda *_: (0,) * len(dims))


def tile(rows):
    return pl.BlockSpec((rows, TILE), lambda j, *_: (0, j))


def pair_of(spec):
    return [spec, spec]


def sigmoid(value):
    return 0.5 * jnp.tanh(0.5 * value) + 0.5


def silu_pair(value):
    sig = sigmoid(value)
    act = value * sig
    return act, sig + act * (1.0 - sig)


def start_or_add(ref, value, first):
    @pl.when(first)
    def _():
        ref[...] = value

    @pl.when(jnp.logical_not(first))
    def _():
        ref[...] += value


def fold(value):
    width = value.shape[1]
    if width % 128:
        return jnp.broadcast_to(
            jnp.sum(value, axis=1, keepdims=True) / 128.0, (value.shape[0], 128)
        )
    return sum(
        value[:, at : at + 128] for at in range(128, width, 128)
    ) + value[:, :128] if width > 128 else value


def rows_of(*folded):
    return jnp.concatenate(
        [jnp.sum(value, axis=1, keepdims=True) for value in folded], axis=1
    ).T


def moments(pre):
    mean = jnp.mean(pre, axis=1, keepdims=True)
    cent = pre - mean
    return jnp.concatenate(
        [mean, jnp.sum(cent * cent, axis=1, keepdims=True)], axis=1
    ).T


def first_kernel(order, counts, factor, mask, w_enc_t, out, high, low):
    del order
    weight = split(w_enc_t[...])
    high[...], low[...] = weight
    scaled = counts[...] * factor[...] * mask[...].T
    out[...] = dot(weight, split(scaled), 1, 0)


def encode_kernel(order, counts, factor, mask, high, low, *outs):
    del order
    scaled = counts[...] * factor[...] * mask[...].T
    product = dot((high[...], low[...]), split(scaled), 1, 0)
    for place, out in enumerate(outs):

        @pl.when(pl.program_id(0) == place)
        def _():
            out[...] = product


def encode_products(order, counts, factor, mask, weight, after=()):
    genes = counts.shape[0]
    hidden = weight[0].shape[0]
    blocks = order.shape[0]
    begin = len(weight) == 1
    matrix = full(hidden, genes)
    return kernel_call(
        first_kernel if begin else encode_kernel,
        (blocks,),
        [
            pl.BlockSpec((genes, TILE), lambda j, order: (0, order[j])),
            pl.BlockSpec((1, TILE), lambda j, order: (0, order[j])),
            full(1, genes),
        ]
        + [matrix] * len(weight),
        [full(hidden, TILE)] * blocks + ([matrix] * 2 if begin else []),
        [shape(hidden, TILE)] * blocks
        + ([shape(hidden, genes, dtype=BF16)] * 2 if begin else []),
        2 * blocks,
        order=order,
        after=after,
    )(counts, factor, mask, *weight)


def prepare_kernel(w_out_t, w_enc_t, out_high, out_low, turn_high, turn_low,
                   enc_high, enc_low):
    out_high[...], out_low[...] = split(w_out_t[...])
    turn_high[...], turn_low[...] = split(w_out_t[...].T)
    enc_high[...], enc_low[...] = split(w_enc_t[...].T)


def prepare(w_out_t, w_enc_t, after):
    hidden, genes = w_out_t.shape
    specs = pair_of(full(hidden, genes)) + pair_of(full(genes, hidden)) * 2
    return kernel_call(
        prepare_kernel,
        (),
        pair_of(full(hidden, genes)),
        specs,
        [shape(hidden, genes, dtype=BF16)] * 2 + [shape(genes, hidden, dtype=BF16)] * 4,
        4,
        after=after,
    )(w_out_t, w_enc_t)


def own_kernel(*refs):
    *parts, pre_out, stats = refs
    pre = sum(part[...] for part in parts[1:]) + parts[0][...]
    pre_out[...] = pre
    stats[...] = moments(pre)


def own_moments(parts):
    rows, columns = parts[0].shape
    return kernel_call(
        own_kernel,
        (),
        [full(rows, columns)] * len(parts),
        [full(rows, columns), full(2, rows)],
        [shape(rows, columns), shape(2, rows)],
        3,
    )(*parts)


def normalize(pre, vector):
    columns = vector.T
    norm = (pre - columns[:, 0:1]) * lax.rsqrt(columns[:, 1:2] + BN_EPS)
    return norm, norm * columns[:, 2:3] + columns[:, 3:4]


def latent_kernel(pre, vector, w_lat, b_lat, noise, z_out):
    _, value = normalize(pre[...], vector[...])
    act, _ = silu_pair(value)
    lat = dot(split(w_lat[...]), split(act), 1, 0) + b_lat[...].T
    latent = noise.shape[0]
    z_out[...] = lat[:latent] + jnp.exp(0.5 * lat[latent:]) * noise[...]


def latent_own(pre, vector, w_lat, b_lat, noise):
    return kernel_call(
        latent_kernel,
        (),
        [full(*a.shape) for a in (pre, vector, w_lat, b_lat, noise)],
        full(*noise.shape),
        shape(*noise.shape),
        3,
    )(pre, vector, w_lat, b_lat, noise)


def spread_kernel(order, w_dec, mine, other, z_all, pre_out, stats):
    blocks = order.shape[1]
    width = mine.shape[2]
    for place in range(blocks):
        spot = order[0, place]
        block = jnp.where(order[1, place] == 0, mine[spot], other[spot])
        z_all[:, place * width : (place + 1) * width] = block
    pre = dot(split(w_dec[...]), split(z_all[...]), 0, 0)
    pre_out[...] = pre
    stats[...] = moments(pre)


def decoder_hidden(order, w_dec, mine, other):
    latent, hidden = w_dec.shape
    cells = order.shape[1] * mine.shape[2]
    return kernel_call(
        spread_kernel,
        (1,),
        [full(latent, hidden), full(*mine.shape), full(*other.shape)],
        [full(latent, cells), full(hidden, cells), full(2, hidden)],
        [shape(latent, cells), shape(hidden, cells), shape(2, hidden)],
        8,
        order=order,
    )(w_dec, mine, other)


def decoder_kernel(cells, order, pre, vector, out_high, out_low, turn_high, turn_low,
                   counts, factor, mask, b_out, w_dec,
                   recon_out, grad_high, grad_low, act_high, act_low, term_out, z_out,
                   sums, bias_out, sum_term, sum_gain, sum_grad):
    del order
    step = pl.program_id(0)
    first = step == 0
    norm, value = normalize(pre[...], vector[...])
    act, slope = silu_pair(value)
    act_pair = split(act)
    act_high[...], act_low[...] = act_pair
    out = dot((turn_high[...], turn_low[...]), act_pair, 1, 0) + b_out[...].T
    recon = jnp.maximum(out, 0.0) + jnp.log(1.0 + jnp.exp(-jnp.abs(out)))
    recon_out[...] = recon
    mask_column = mask[...].T * (1.0 / cells)
    grad = (recon - counts[...] * factor[...]) * (mask_column * sigmoid(out))
    grad_pair = split(grad)
    grad_high[...], grad_low[...] = grad_pair
    term = dot((out_high[...], out_low[...]), grad_pair, 1, 0) * slope
    term_out[...] = term
    scaled_dec = w_dec[...] * (vector[2:3, :] * lax.rsqrt(vector[1:2, :] + BN_EPS))
    z_out[...] = dot(split(scaled_dec), split(term), 1, 0)
    start_or_add(sum_term, fold(term), first)
    start_or_add(sum_gain, fold(term * norm), first)
    start_or_add(sum_grad, fold(grad), first)

    @pl.when(step == pl.num_programs(0) - 1)
    def _():
        sums[...] = rows_of(sum_term[...], sum_gain[...])
        bias_out[...] = rows_of(sum_grad[...])


def decoder(cells, order, pre, vector, out_pair, turn_pair, counts, factor, mask, b_out,
            w_dec):
    hidden, genes = out_pair[0].shape
    here = counts.shape[1]
    latent = w_dec.shape[0]
    return kernel_call(
        lambda *refs: decoder_kernel(cells, *refs),
        (here // TILE,),
        [tile(hidden), full(4, hidden)]
        + pair_of(full(hidden, genes))
        + pair_of(full(genes, hidden))
        + [
            tile(genes),
            tile(1),
            full(1, genes),
            full(1, genes),
            full(latent, hidden),
        ],
        [tile(genes)]
        + pair_of(tile(genes))
        + pair_of(tile(hidden))
        + [
            tile(hidden),
            pl.BlockSpec((latent, TILE), lambda j, order: (0, order[j])),
            full(2, hidden),
            full(1, genes),
        ],
        [shape(genes, here)]
        + [shape(genes, here, dtype=BF16)] * 2
        + [shape(hidden, here, dtype=BF16)] * 2
        + [
            shape(hidden, here),
            shape(latent, here),
            shape(2, hidden),
            shape(1, genes),
        ],
        40,
        order=order,
        scratch=[
            pltpu.VMEM((hidden, 128), F32),
            pltpu.VMEM((hidden, 128), F32),
            pltpu.VMEM((genes, 128), F32),
        ],
    )(pre, vector, *out_pair, *turn_pair, counts, factor, mask, b_out, w_dec)


def weight_kernel(order, left_high, left_low, right_high, right_low, out):
    del order
    product = dot(
        (left_high[...], left_low[...]), (right_high[...], right_low[...]), 1, 1
    )
    start_or_add(out, product, pl.program_id(0) == 0)


def weight_half(order, halves, left, right, width, after=()):
    rows, here = left[0].shape
    rows //= halves
    genes = right[0].shape[0]
    return kernel_call(
        weight_kernel,
        (here // width,),
        pair_of(pl.BlockSpec((rows, width), lambda j, order: (order[0], j)))
        + pair_of(pl.BlockSpec((genes, width), lambda j, order: (0, j))),
        full(rows, genes),
        shape(rows, genes),
        14 // halves,
        order=order,
        after=after,
    )(*left, *right)


def small_weight_kernel(z, pre, vector, term, term_out, pair_out, sum_out):
    first = pl.program_id(0) == 0
    norm, _ = normalize(pre[...], vector[...])
    z_pair = split(z[...])
    start_or_add(term_out, dot(z_pair, split(term[...]), 1, 1), first)
    start_or_add(pair_out, dot(z_pair, split(norm), 1, 1), first)
    start_or_add(sum_out, rows_of(z[...]), first)


def small_weights(z, pre, vector, term, after=()):
    hidden, here = pre.shape
    latent = z.shape[0]
    return kernel_call(
        small_weight_kernel,
        (here // TILE,),
        [tile(latent), tile(hidden), full(4, hidden), tile(hidden)],
        [full(latent, hidden)] * 2 + [full(1, latent)],
        [shape(latent, hidden)] * 2 + [shape(1, latent)],
        12,
        after=after,
    )(z, pre, vector, term)


def again_kernel(cells, pre_enc, vector1, w_lat, b_lat, pre_dec, vector2, sums2, w_dec,
                 lat_out, act_out, slope_out, fix_out):
    _, value = normalize(pre_enc[...], vector1[...])
    act, slope = silu_pair(value)
    act_out[...] = act
    slope_out[...] = slope
    lat_out[...] = dot(split(w_lat[...]), split(act), 1, 0) + b_lat[...].T
    norm2, _ = normalize(pre_dec[...], vector2[...])
    scaled_dec = w_dec[...] * (vector2[2:3, :] * lax.rsqrt(vector2[1:2, :] + BN_EPS))
    gain_term = scaled_dec * (sums2[1:2, :] * (1.0 / cells))
    shift_term = jnp.sum(
        scaled_dec * (sums2[0:1, :] * (1.0 / cells)), axis=1, keepdims=True
    )
    fix_out[...] = dot(split(gain_term), split(norm2), 1, 0) + shift_term


def encode_again(cells, pre_enc, vector1, w_lat, b_lat, pre_dec, vector2, sums2, w_dec,
                 after=()):
    hidden, here = pre_enc.shape
    latents = w_lat.shape[0]
    latent = w_dec.shape[0]
    return kernel_call(
        lambda *refs: again_kernel(cells, *refs),
        (here // TILE,),
        [
            tile(hidden),
            full(4, hidden),
            full(latents, hidden),
            full(1, latents),
            tile(hidden),
            full(4, hidden),
            full(2, hidden),
            full(latent, hidden),
        ],
        [tile(latents), tile(hidden), tile(hidden), tile(latent)],
        [
            shape(latents, here),
            shape(hidden, here),
            shape(hidden, here),
            shape(latent, here),
        ],
        16,
        after=after,
    )(pre_enc, vector1, w_lat, b_lat, pre_dec, vector2, sums2, w_dec)


def latent_back_kernel(cells, order, mine, other, fix, lat, noise, w_lat, slope, act, pre,
                       vector, grad_out, sums, weight_out, bias_out,
                       sum_grad, sum_gain, sum_lat):
    step = pl.program_id(0)
    first = step == 0
    latent = noise.shape[0]
    term_z = jnp.where(order[1, step] == 0, mine[...], other[...])
    grad_z = term_z - fix[...]
    mu = lat[:latent, :]
    spread = jnp.exp(0.5 * lat[latent:, :])
    grad_mu = grad_z + (ALPHA / cells) * mu
    grad_logvar = 0.5 * grad_z * noise[...] * spread + (0.5 * ALPHA / cells) * (
        spread * spread - 1.0
    )
    grad_lat = jnp.concatenate([grad_mu, grad_logvar], axis=0)
    lat_pair = split(grad_lat)
    grad_in = dot(split(w_lat[...]), lat_pair, 0, 0) * slope[...]
    grad_out[...] = grad_in
    norm, _ = normalize(pre[...], vector[...])
    start_or_add(sum_grad, fold(grad_in), first)
    start_or_add(sum_gain, fold(grad_in * norm), first)
    start_or_add(sum_lat, fold(grad_lat), first)
    start_or_add(weight_out, dot(lat_pair, split(act[...]), 1, 1), first)

    @pl.when(step == pl.num_programs(0) - 1)
    def _():
        sums[...] = rows_of(sum_grad[...], sum_gain[...])
        bias_out[...] = rows_of(sum_lat[...])


def latent_back(cells, order, mine, other, fix, lat, noise, w_lat, slope, act, pre, vector):
    hidden, here = pre.shape
    latents = lat.shape[0]
    latent = noise.shape[0]
    block = pl.BlockSpec((None, latent, TILE), lambda j, order: (order[0, j], 0, 0))
    return kernel_call(
        lambda *refs: latent_back_kernel(cells, *refs),
        (here // TILE,),
        [
            block,
            block,
            tile(latent),
            tile(latents),
            tile(latent),
            full(latents, hidden),
            tile(hidden),
            tile(hidden),
            tile(hidden),
            full(4, hidden),
        ],
        [tile(hidden), full(2, hidden), full(latents, hidden), full(1, latents)],
        [
            shape(hidden, here),
            shape(2, hidden),
            shape(latents, hidden),
            shape(1, latents),
        ],
        16,
        order=order,
        scratch=[
            pltpu.VMEM((hidden, 128), F32),
            pltpu.VMEM((hidden, 128), F32),
            pltpu.VMEM((latents, 128), F32),
        ],
    )(mine, other, fix, lat, noise, w_lat, slope, act, pre, vector)


def encoder_weight_kernel(cells, order, grad_in, pre, vector, counts, factor, mask,
                          high, low, out):
    del order
    columns = vector[...].T
    scale = lax.rsqrt(columns[:, 1:2] + BN_EPS)
    norm = (pre[...] - columns[:, 0:1]) * scale
    grad_pre = (columns[:, 2:3] * scale) * (
        grad_in[...]
        - columns[:, 4:5] * (1.0 / cells)
        - norm * (columns[:, 5:6] * (1.0 / cells))
    )
    pair = split(grad_pre)
    high[...], low[...] = pair
    scaled = counts[...] * factor[...] * mask[...].T
    product = dot(pair, split(scaled), 1, 1)
    start_or_add(out, product, pl.program_id(0) == 0)


def encoder_weight(cells, order, halves, grad_in, pre, vector, sums, counts, factor, mask,
                   width, after=()):
    hidden, here = pre.shape
    rows = hidden // halves
    genes = counts.shape[0]
    parts = pl.BlockSpec((rows, width), lambda j, order: (order[0], j))
    vectors = jnp.concatenate([vector, sums])
    vectors = vectors.reshape(6, halves, rows).swapaxes(0, 1)
    mine = pl.BlockSpec((rows, width), lambda j, order: (0, j))
    return kernel_call(
        lambda *refs: encoder_weight_kernel(cells, *refs),
        (here // width,),
        [
            parts,
            parts,
            pl.BlockSpec((None, 6, rows), lambda j, order: (order[0], 0, 0)),
            pl.BlockSpec((genes, width), lambda j, order: (0, j)),
            pl.BlockSpec((1, width), lambda j, order: (0, j)),
            full(1, genes),
        ],
        pair_of(mine) + [full(rows, genes)],
        [shape(rows, here, dtype=BF16)] * 2 + [shape(rows, genes)],
        18 // halves,
        order=order,
        after=after,
    )(grad_in, pre, vectors, counts, factor, mask)


def counts_kernel(cells, halves, order, *refs):
    enc_high, enc_low, *grads, recon, counts, factor, mask, out = refs
    mask_column = mask[...].T
    weight = factor[...] * mask_column
    diff = (recon[...] - counts[...] * factor[...]) * (mask_column * (1.0 / cells))
    pairs = [(grads[2 * k][...], grads[2 * k + 1][...]) for k in range(halves)]
    if halves == 2:
        swapped = order[0] != 0
        pairs = [
            tuple(jnp.where(swapped, b, a) for a, b in zip(*pairs)),
            tuple(jnp.where(swapped, a, b) for a, b in zip(*pairs)),
        ]
        pairs = [tuple(jnp.concatenate([a, b], axis=0) for a, b in zip(*pairs))]
    out[...] = (dot((enc_high[...], enc_low[...]), pairs[0], 1, 0) - diff) * weight


def counts_back(cells, order, enc_pair, grads, recon, counts, factor, mask, after=()):
    genes, hidden = enc_pair[0].shape
    here = counts.shape[1]
    halves = len(grads)
    return kernel_call(
        lambda *refs: counts_kernel(cells, halves, *refs),
        (here // TILE,),
        pair_of(full(genes, hidden))
        + pair_of(tile(hidden // halves)) * halves
        + [tile(genes), tile(genes), tile(1), full(1, genes)],
        tile(genes),
        shape(genes, here),
        18,
        order=order,
        after=after,
    )(*enc_pair, *[x for pair in grads for x in pair], recon, counts, factor, mask)


def add_kernel(left, right, out):
    out[...] = left[...] + right[...]


def add_arrays(left, right, after=()):
    rows, columns = left.shape
    return kernel_call(
        add_kernel,
        (2,),
        pair_of(pl.BlockSpec((rows // 2, columns), lambda j: (j, 0))),
        pl.BlockSpec((rows // 2, columns), lambda j: (j, 0)),
        shape(rows, columns),
        1,
        after=after,
    )(left, right)


def join_kernel(order, mine, other, out):
    own = order[0] == pl.program_id(0)

    @pl.when(own)
    def _():
        out[...] = other[...]

    @pl.when(jnp.logical_not(own))
    def _():
        out[...] = mine[...]


def join_halves(order, mine, other):
    rows, columns = mine.shape
    return kernel_call(
        join_kernel,
        (2,),
        pair_of(full(rows, columns)),
        pl.BlockSpec((rows, columns), lambda j, _: (j, 0)),
        shape(2 * rows, columns),
        2,
        order=order,
    )(mine, other)


def swap(value, axis, bit):
    size = lax.axis_size(axis)
    return lax.ppermute(value, axis, [(i, i ^ bit) for i in range(size)])


def bits(axis):
    size, bit, out = lax.axis_size(axis), 1, []
    while bit < size:
        out.append(bit)
        bit *= 2
    return out


def add_all(value, axes):
    for axis in axes:
        for bit in bits(axis):
            value = value + swap(value, axis, bit)
    return value


def moments_all(both, count, axes):
    for axis in axes:
        for bit in bits(axis):
            other = swap(both, axis, bit)
            gap = both[0] - other[0]
            both = jnp.stack(
                [
                    0.5 * (both[0] + other[0]),
                    both[1] + other[1] + gap * gap * (0.5 * count),
                ]
            )
            count = 2 * count
    return both[0], both[1] / count


def scatter_gene_blocks(value):
    me = lax.axis_index(GENE)
    for bit in reversed(bits(GENE)):
        half = value.shape[0] // 2
        upper = (me & bit) != 0
        sent = jnp.where(upper, value[:half], value[half:])
        kept = jnp.where(upper, value[half:], value[:half])
        value = kept + swap(sent, GENE, bit)
    return value[0]


def gene_pairs(links):
    return [(2 * a + y, 2 * b + y) for a, b in links for y in (0, 1)]


OUTER = gene_pairs([(0, 1), (3, 2)])
MIDDLE = gene_pairs([(1, 2), (2, 1)])
SIDES = gene_pairs([(0, 1), (1, 0), (2, 3), (3, 2)])


def line_order(z):
    low = z < 2
    return [
        jnp.where(low, z + 3, z + 1) % 4,
        (z + 2) % 4,
        jnp.where(low, z + 1, z + 3) % 4,
        z,
    ]


def scatter_encoded(counts, factor, mask, w_enc_t, w_out_t):
    size = lax.axis_size(GENE)
    here = counts.shape[1]
    me = lax.axis_index(GENE)
    if size != 8 or here != size * TILE:
        order = jnp.arange(here // TILE, dtype=jnp.int32)
        one, *pair = encode_products(order[:1], counts, factor, mask, [w_enc_t])
        blocks = [one] + list(encode_products(order[1:], counts, factor, mask, pair))
        return [
            lax.psum_scatter(
                jnp.concatenate(blocks, axis=1), GENE, scatter_dimension=1, tiled=True
            )
        ], prepare(w_out_t, w_enc_t, ())
    z, y = me // 2, me % 2
    order = jnp.stack(
        [2 * spot + side for spot in line_order(z) for side in (1 - y, y)]
    ).astype(jnp.int32)
    one, *pair = encode_products(order[:1], counts, factor, mask, [w_enc_t])
    blocks = [one]
    blocks += encode_products(order[1:3], counts, factor, mask, pair)
    blocks += encode_products(order[3:], counts, factor, mask, pair, after=blocks[1:2])
    weights = prepare(w_out_t, w_enc_t, blocks[3:4])
    part = [blocks[2 * k + 1] + swap(blocks[2 * k], GENE, 1) for k in range(4)]
    middle = (z == 1) | (z == 2)
    first = lax.ppermute(part[0], GENE, OUTER)
    second = lax.ppermute(part[1], GENE, OUTER)
    across = lax.ppermute(part[1] + first, GENE, MIDDLE)
    side = lax.ppermute(jnp.where(middle, part[0] + across, part[2]), GENE, SIDES)
    inner = lax.ppermute(part[2] + second, GENE, MIDDLE)
    return [part[3], side, inner], weights


def on_line(value):
    return lax.axis_size(GENE) == 8 and value.shape[1] == TILE


def gather_blocks(value):
    rows = value.shape[0]
    if not on_line(value):
        value = lax.all_gather(value, GENE, axis=1, tiled=True)
        blocks = value.shape[1] // TILE
        stack = jnp.moveaxis(value.reshape(rows, blocks, TILE), 1, 0)
        place = jnp.arange(blocks, dtype=jnp.int32)
        return stack, stack, jnp.stack([place, 0 * place])
    mine = jnp.stack([value] + [swap(value, GENE, bit) for bit in (2, 4, 6)])
    other = swap(mine, GENE, 1)
    rank = lax.axis_index(GENE) ^ jnp.arange(8, dtype=jnp.int32)
    return mine, other, jnp.stack([rank // 2, rank % 2]).astype(jnp.int32)


def send_order(here):
    if lax.axis_size(GENE) != 8 or here != 8 * TILE:
        return jnp.arange(here // TILE, dtype=jnp.int32)
    rank = lax.axis_index(GENE) ^ jnp.arange(8, dtype=jnp.int32)
    return (4 * (1 - rank % 2) + (rank // 2 + 3) % 4).astype(jnp.int32)


def scatter_terms(value):
    size = lax.axis_size(GENE)
    here = value.shape[1]
    if size != 8 or here != size * TILE:
        return lax.psum_scatter(value, GENE, scatter_dimension=1, tiled=True)
    half = here // 2
    part = value[:, half:] + swap(value[:, :half], GENE, 1)
    total = part[:, 3 * TILE :]
    for k in (1, 2, 3):
        total = total + swap(part[:, (k - 1) * TILE : k * TILE], GENE, 2 * k)
    return total


def add_batch_halves(order, halves, after=()):
    if len(halves) == 1:
        return lax.psum(halves[0], BATCH)
    other, mine = halves
    mine = add_arrays(mine, swap(other, BATCH, 1))
    mine = add_arrays(mine, swap(mine, BATCH, 2), after)
    other = swap(mine, BATCH, 1)
    return join_halves(order, mine, other)


def on_device(
    counts_in,
    umi_total,
    gene_mask,
    noise,
    w_enc,
    gain_enc,
    shift_enc,
    w_lat,
    b_lat,
    w_dec,
    gain_dec,
    shift_dec,
    w_out,
    b_out,
    mean_enc,
    var_enc,
    mean_dec,
    var_dec,
):
    here = counts_in.shape[1]
    cells = here * lax.axis_size(BATCH)
    hidden = w_enc.shape[1]
    ranks = lax.axis_size(GENE)
    share = hidden // ranks
    own = here // ranks
    latent = noise.shape[0]
    me = lax.axis_index(GENE)
    both = (BATCH, GENE)
    core = lax.axis_index(BATCH) % 2
    halves = 2 if lax.axis_size(BATCH) == 4 else 1
    order = [1 - core, core] if halves == 2 else [0 * core]
    order = [half.astype(jnp.int32)[None] for half in order]
    width = 1024

    def hidden_part(vector):
        return lax.dynamic_slice_in_dim(vector, me * share, share, vector.ndim - 1)

    def hidden_whole(part):
        empty = jnp.zeros((part.shape[0], hidden), F32)
        return add_all(
            lax.dynamic_update_slice_in_dim(empty, part, me * share, 1), (GENE,)
        )

    factor = (UMI_SCALE / umi_total.astype(F32))[None, :]
    mask = gene_mask.astype(F32)[None, :]
    w_enc_t = w_enc.T
    w_out_t = w_out.T
    b_lat_row = b_lat[None, :]
    noise_own = lax.dynamic_slice_in_dim(noise, me * own, own, 1)

    parts, weights = scatter_encoded(counts_in, factor, mask, w_enc_t, w_out_t)
    out_pair, turn_pair, enc_pair = weights[:2], weights[2:4], weights[4:]
    affine1 = hidden_whole(jnp.stack([gain_enc, shift_enc]))
    pre_own, stats1 = own_moments(parts)
    pre_enc = lax.all_gather(pre_own, GENE, axis=1, tiled=True)
    mean1, var1 = moments_all(stats1, own, both)
    vector1 = jnp.concatenate([mean1[None], var1[None], affine1])
    z_own = latent_own(pre_own, vector1, w_lat, b_lat_row, noise_own)

    z_mine, z_other, z_order = gather_blocks(z_own)
    z, pre_dec, stats2 = decoder_hidden(z_order, w_dec, z_mine, z_other)
    mean2, var2 = moments_all(stats2, here, (BATCH,))
    vector2 = jnp.stack([mean2, var2, gain_dec, shift_dec])
    recon, grad_high, grad_low, act_high, act_low, term, term_z, sums2, grad_b_out = decoder(
        cells, send_order(here), pre_dec, vector2, out_pair, turn_pair, counts_in, factor,
        mask, b_out[None, :], w_dec
    )

    term_mine, term_other, term_order = gather_blocks(scatter_terms(term_z))
    sums2 = add_all(sums2, both)
    grad_w_out = [
        weight_half(half, halves, (act_high, act_low), (grad_high, grad_low), width)
        for half in order
    ]
    grad_w_out = add_batch_halves(order[0], grad_w_out).T
    lat, act1, slope1, fix_z = encode_again(
        cells, pre_enc, vector1, w_lat, b_lat_row, pre_dec, vector2, sums2, w_dec
    )
    term_w_dec, pair_w_dec, sum_z = small_weights(z, pre_dec, vector2, term)

    grad_in1, sums1, grad_w_lat, grad_b_lat = latent_back(
        cells, term_order, term_mine, term_other, fix_z, lat, noise, w_lat, slope1, act1,
        pre_enc, vector1
    )
    sums1 = add_all(
        jnp.concatenate(
            [sums1.reshape(-1), grad_b_lat[0], grad_b_out[0], sum_z[0]]
        ),
        (BATCH,),
    )
    grad_b_lat = sums1[2 * hidden : 2 * hidden + 2 * latent]
    grad_b_out = sums1[2 * hidden + 2 * latent : -latent]
    sum_z = sums1[-latent:]
    sums1 = sums1[: 2 * hidden].reshape(2, hidden)
    grads, weight_parts, last = [], [], ()
    for half in order:
        high, low, part = encoder_weight(
            cells, half, halves, grad_in1, pre_enc, vector1, sums1, counts_in, factor, mask,
            width, after=last
        )
        grads.append((high, low))
        weight_parts.append(part)
        last = (part,)
    grad_counts = counts_back(
        cells, order[0], enc_pair, grads, recon, counts_in, factor, mask
    )
    grad_w_enc = add_batch_halves(order[0], weight_parts, (grad_counts,)).T

    term_w_dec = scatter_gene_blocks(
        jnp.moveaxis(term_w_dec.reshape(latent, ranks, share), 1, 0)
    )
    small = add_all(
        jnp.concatenate(
            [
                term_w_dec,
                hidden_part(pair_w_dec),
                hidden_part(grad_w_lat),
            ]
        ),
        (BATCH,),
    )
    term_w_dec = small[:latent]
    pair_w_dec = small[latent : 2 * latent]
    grad_w_lat = small[2 * latent :]
    scale2 = hidden_part(gain_dec * lax.rsqrt(var2 + BN_EPS))
    grad_shift2 = hidden_part(sums2[0])
    grad_gain2 = hidden_part(sums2[1])
    grad_w_dec = scale2[None, :] * (
        term_w_dec
        - sum_z[:, None] * (grad_shift2 / cells)[None, :]
        - pair_w_dec * (grad_gain2 / cells)[None, :]
    )

    correct = cells / (cells - 1.0)
    new_mean_enc = (1.0 - MOMENTUM) * mean_enc + MOMENTUM * hidden_part(mean1)
    new_var_enc = (1.0 - MOMENTUM) * var_enc + MOMENTUM * hidden_part(var1) * correct
    new_mean_dec = (1.0 - MOMENTUM) * mean_dec + MOMENTUM * mean2
    new_var_dec = (1.0 - MOMENTUM) * var_dec + MOMENTUM * var2 * correct
    return (
        recon,
        grad_counts,
        grad_w_enc,
        hidden_part(sums1[1]),
        hidden_part(sums1[0]),
        grad_w_lat,
        grad_b_lat,
        grad_w_dec,
        grad_gain2,
        grad_shift2,
        grad_w_out,
        grad_b_out,
        new_mean_enc,
        new_var_enc,
        new_mean_dec,
        new_var_dec,
    )


def solution(mesh):
    return jax.shard_map(
        on_device,
        mesh=mesh,
        in_specs=(
            P(GENE, BATCH),
            P(BATCH),
            P(GENE),
            P(None, BATCH),
            P(GENE, None),
            P(GENE),
            P(GENE),
            P(),
            P(),
            P(),
            P(),
            P(),
            P(GENE, None),
            P(GENE),
            P(GENE),
            P(GENE),
            P(),
            P(),
        ),
        out_specs=(
            P(GENE, BATCH),
            P(GENE, BATCH),
            P(GENE, None),
            P(GENE),
            P(GENE),
            P(None, GENE),
            P(),
            P(None, GENE),
            P(GENE),
            P(GENE),
            P(GENE, None),
            P(GENE),
            P(GENE),
            P(GENE),
            P(),
            P(),
        ),
        check_vma=False,
    )
```

time: 962 us -> 490 us (0.51)
  blocking collectives: 319 us -> 0 us
  Pallas kernels: 0 us -> 247 us
  waiting for transfers between devices: 329 us -> 108 us
  matrix products: 204 us -> 0 us
  starting transfers between devices: 4.5 us -> 68.1 us
  local copies, waits for them, and re-layouts: 58 us -> 23.1 us
    unnamed x2 -> x0, blocking collectives: 277 us -> none
    pallas_call x0 -> x22, Pallas kernels: none -> 247 us  [kernel_call(): return lambda *args: call(*prefetch, *args, *after)]
    dot_general x12 -> x0, matrix products: 204 us -> none  [contract(): lax.dot_general(left, right, (((left_dim,), (right_dim,)), ((), ())), pre...]
    all_gather x2 -> x1, waiting for transfers between devices: 185 us -> 0.01 us  [on_device(): pre_enc = lax.all_gather(pre_own, GENE, axis=1, tiled=True)]
    psum x2 -> x0, waiting for transfers between devices: 135 us -> none  [the longest x1 76.9 us: on_device(): grad_z = lax.psum(contract(dec_cols, grad_pre_dec, 1, 0), 'gene')]
    ppermute x0 -> x49, waiting for transfers between devices: none -> 108 us  [the longest x44 93.8 us: swap(): return lax.ppermute(value, axis, [(i, i ^ bit) for i in range(size)])]
    ppermute x0 -> x49, starting transfers between devices: none -> 68.1 us  [the longest x44 51.4 us: swap(): return lax.ppermute(value, axis, [(i, i ^ bit) for i in range(size)])]
    unnamed x77 -> x60, local copies, waits for them, and re-layouts: 58 us -> 9.98 us
  transfers between devices with their start and end apart: 6 -> 50, of which waited for: 6 -> 28; matrix products, arithmetic and copies ran while one was open for 9% -> 7% of each run, Pallas kernels for 0% -> 48%
where the time goes in v1:
time: 490 us; the launch traced here: 483 us
  Pallas kernels  247 us (50%)
  waiting for transfers between devices  108 us (22%)
  starting transfers between devices  68.1 us (14%)
  local copies, waits for them, and re-layouts  23.1 us (5%)
  other arithmetic  22.5 us (5%)
  between operations  15 us (3%)
    pallas_call x22, Pallas kernels, kernel_call(): return lambda *args: call(*prefetch, *args, *after)  247 us
    ppermute x44, waiting for transfers between devices, swap(): return lax.ppermute(value, axis, [(i, i ^ bit) for i in range(size)])  93.8 us
    ppermute x44, starting transfers between devices, swap(): return lax.ppermute(value, axis, [(i, i ^ bit) for i in range(size)])  51.4 us
    unnamed x60, local copies, waits for them, and re-layouts  9.98 us
  transfers between devices with their start and end apart: 50, of which 28 were waited for; matrix products, arithmetic and copies ran while one was open for 7% of the time, Pallas kernels for 48%

profile of v1, /device:TPU:0, one launch (start us, length us, event | category | flops | bytes accessed | tf_op | source)
XLA Modules:
  0.0 483.1 jit_solution(14227509674409377584)
XLA Ops:
  9.8 4.8 shard_map.297
  18.1 7.5 %shard_map.298 = (f32[800,256]{1,0:T(8,128)}, f32[800,256]{1,0:T(8,128)}) custom-call(s32[2]{0:T(128)} %pad_add_fusion.1.refs_0_, f32[896,2048]{1,0:T(8,128)} %refs_8_.1, f32[1,2048]{1,0:T(1,128)} %bitcast.64, f32[1,896]{1,0:T(1,128)} %broadcast_in_dim.27.refs_3_.refs_9_.refs_6_.refs_10_, bf16[800,896]{1,0:T(8,128)(2,1)} %get-tuple-element.63.refs_4_, ...), custom_call_target="tpu_custom_call" | custom-call | flops 4400000000 | bytes 1024 | tf_op jit(solution)/shard_map/pallas_call | solution.py:69
  26.2 10.6 %collective-permute-done.1 = f32[800,256]{1,0:T(8,128)S(1)} collective-permute-done((f32[800,256]{1,0:T(8,128)}, f32[800,256]{1,0:T(8,128)S(1)}, u32[]{:S(2)}, u32[]{:S(2)}) %collective-permute-start.1) | collective-permute-done | bytes 819232 | tf_op jit(solution)/shard_map/ppermute | solution.py:630
  42.2 13.7 %shard_map.299 = (f32[800,256]{1,0:T(8,128)}, f32[800,256]{1,0:T(8,128)}, f32[800,256]{1,0:T(8,128)}, f32[800,256]{1,0:T(8,128)}, f32[800,256]{1,0:T(8,128)}) custom-call(s32[5]{0:T(128)} %stack.119.refs_0_, f32[896,2048]{1,0:T(8,128)} %refs_8_.1, f32[1,2048]{1,0:T(1,128)} %bitcast.65, f32[1,896]{1,0:T(1,128)} %broadcast_in_dim.27.refs_3_.refs_9_.refs_6_.refs_10_, ...), custom_call_target="tpu_custom_call" | custom-call | flops 11000000512 | bytes 1024 | tf_op jit(solution)/shard_map/pallas_call | solution.py:69
  60.8 8.1 %collective-permute-start.7 = (f32[800,256]{1,0:T(8,128)}, f32[800,256]{1,0:T(8,128)}, u32[]{:S(2)}, u32[]{:S(2)}) collective-permute-start(f32[800,256]{1,0:T(8,128)} %get-tuple-element.118), channel_id=1, source_target_pairs={{0,2},{1,3},{6,4},{7,5},{8,10},{9,11},{14,12},{15,13},{16,18},{17,... | collective-permute-start | bytes 2457608 | tf_op jit(solution)/shard_map/ppermute | solution.py:718
  70.4 6.9 %collective-permute-done.5 = f32[800,256]{1,0:T(8,128)} collective-permute-done((f32[800,256]{1,0:T(8,128)}, f32[800,256]{1,0:T(8,128)}, u32[]{:S(2)}, u32[]{:S(2)}) %collective-permute-start.5) | collective-permute-done | bytes 819232 | tf_op jit(solution)/shard_map/ppermute | solution.py:630
  77.3 5.2 %collective-permute-done.7 = f32[800,256]{1,0:T(8,128)} collective-permute-done((f32[800,256]{1,0:T(8,128)}, f32[800,256]{1,0:T(8,128)}, u32[]{:S(2)}, u32[]{:S(2)}) %collective-permute-start.7) | collective-permute-done | bytes 819232 | tf_op jit(solution)/shard_map/ppermute | solution.py:718
  92.3 8.7 %collective-permute-done.6.refs_1_ = f32[800,256]{1,0:T(8,128)S(1)} collective-permute-done((f32[800,256]{1,0:T(8,128)S(1)}, f32[800,256]{1,0:T(8,128)S(1)}, u32[]{:S(2)}, u32[]{:S(2)}) %collective-permute-start.6) | collective-permute-done | bytes 819232 | tf_op jit(solution)/shard_map/ppermute | solution.py:720
  140.9 7.8 %shard_map.303 = (bf16[800,896]{1,0:T(8,128)(2,1)}, bf16[800,896]{1,0:T(8,128)(2,1)}, bf16[896,800]{1,0:T(8,128)(2,1)}, bf16[896,800]{1,0:T(8,128)(2,1)}, bf16[8...) custom-call(f32[800,896]{1,0:T(8,128)} %bitcast.76, f32[800,896]{1,0:T(8,128)} %bitcast.54, f32[800,256]{1,0:T(8,128)} %get-tuple-element.69.refs_2_), custom_call_target="tpu_custom_call" | custom-call | flops 4400000000 | bytes 1024 | tf_op jit(solution)/shard_map/pallas_call | solution.py:69
  148.7 6.5 %collective-permute-done.20.refs_3_ = f32[4,100,256]{2,1,0:T(8,128)S(1)} collective-permute-done((f32[4,100,256]{2,1,0:T(8,128)S(1)}, f32[4,100,256]{2,1,0:T(8,128)S(1)}, u32[]{:S(2)}, u32[]{:S(2)}) %collective-permute-start.20) | collective-permute-done | bytes 409632 | tf_op jit(solution)/shard_map/ppermute | solution.py:630
  156.0 8.0 %shard_map.302 = (f32[100,2048]{1,0:T(8,128)}, f32[800,2048]{1,0:T(8,128)}, f32[2,800]{1,0:T(2,128)}) custom-call(s32[2,8]{1,0:T(2,128)} %pad_add_fusion.refs_0_, f32[100,800]{1,0:T(8,128)} %refs_7_.3, f32[4,100,256]{2,1,0:T(8,128)} %copy-done.8, f32[4,100,256]{2,1,0:T(8,128)} %copy-done.29), custom_call_target="tpu_custom_call" | custom-call | flops 8800000000 | bytes 1024 | tf_op jit(solution)/shard_map/pallas_call | solution.py:69
  171.2 63.6 %shard_map.304 = (f32[896,2048]{1,0:T(8,128)}, bf16[896,2048]{1,0:T(8,128)(2,1)}, bf16[896,2048]{1,0:T(8,128)(2,1)}, bf16[800,2048]{1,0:T(8,128)(2,1)}, bf16[800...) custom-call(s32[8]{0:T(128)} %fusion.13.refs_0_, ...), custom_call_target="tpu_custom_call" | custom-call | flops 44000002048 | bytes 1024 | tf_op jit(solution)/shard_map/pallas_call | solution.py:69
  234.8 9.4 %shard_map.315 = f32[400,896]{1,0:T(8,128)} custom-call(s32[1]{0:T(128)} %bitcast.18.refs_0_, bf16[800,2048]{1,0:T(8,128)(2,1)} %get-tuple-element.106.refs_1_, bf16[800,2048]{1,0:T(8,128)(2,1)} %get-tuple-element.107.refs_2_, bf16[896,2048]{1,0:T(8,128)(2,1)} %get-tuple-element.108.refs_3_, bf16[896,2048]{1,0:T(8,128)(2,1)} %get-tuple-element.109.refs_4_), custom_call_target="tpu_custom_call" | custom-call | flops 7699999744 | bytes 1024 | tf_op jit(solution)/shard_map/pallas_call | solution.py:69
  244.8 14.7 %shard_map.307 = (f32[100,800]{1,0:T(8,128)}, f32[100,800]{1,0:T(8,128)}, f32[1,100]{1,0:T(1,128)}) custom-call(f32[100,2048]{1,0:T(8,128)} %get-tuple-element.94.refs_0_, f32[800,2048]{1,0:T(8,128)} %get-tuple-element.75.refs_1_.refs_4_, f32[4,800]{1,0:T(4,128)} %pad_maximum_fusion.4.refs_2_.refs_5_, f32[800,2048]{1,0:T(8,128)} %get-tuple-element.95.refs_3_), custom_call_target="tpu_custom_call" | custom-call | flops 13200000000 | bytes 1024 | tf_op jit(solution)/shard_map/pallas_call | solution.py:69
  259.5 9.6 %shard_map.314.refs_0_ = f32[400,896]{1,0:T(8,128)} custom-call(s32[1]{0:T(128)} %bitcast.26.refs_0_, bf16[800,2048]{1,0:T(8,128)(2,1)} %get-tuple-element.106.refs_1_, bf16[800,2048]{1,0:T(8,128)(2,1)} %get-tuple-element.107.refs_2_, bf16[896,2048]{1,0:T(8,128)(2,1)} %get-tuple-element.108.refs_3_, bf16[896,2048]{1,0:T(8,128)(2,1)} %get-tuple-element.109.refs_4_), custom_call_target="tpu_custom_call" | custom-call | flops 7699999744 | bytes 1024 | tf_op jit(solution)/shard_map/pallas_call | solution.py:69
  277.5 8.5 %collective-permute-done.33 = f32[2,800]{1,0:T(2,128)S(1)} collective-permute-done((f32[2,800]{1,0:T(2,128)S(1)}, f32[2,800]{1,0:T(2,128)S(1)}, u32[]{:S(2)}, u32[]{:S(2)}) %collective-permute-start.33) | collective-permute-done | bytes 6432 | tf_op jit(solution)/shard_map/ppermute | solution.py:630
  315.3 17.4 %shard_map.305 = (f32[200,2048]{1,0:T(8,128)}, f32[800,2048]{1,0:T(8,128)}, f32[800,2048]{1,0:T(8,128)}, f32[100,2048]{1,0:T(8,128)}) custom-call(f32[800,2048]{1,0:T(8,128)} %all-gather.2.cloned.1.call-done.refs_0_.refs_9_.refs_2_, f32[4,800]{1,0:T(4,128)} %pad_maximum_fusion.3.refs_1_.refs_10_, f32[200,800]{1,0:T(8,128)} %refs_6_.1, f32[1,200]{1,0:T(1,128)} %bitcast.78, ...), custom_call_target="tpu_custom_call" | custom-call | flops 17600000000 | bytes 1024 | tf_op jit(solution)/shard_map/pallas_call | solution.py:69
  333.5 21.9 %shard_map.306 = (f32[800,2048]{1,0:T(8,128)}, f32[2,800]{1,0:T(2,128)}, f32[200,800]{1,0:T(8,128)}, f32[1,200]{1,0:T(1,128)}) custom-call(s32[2,8]{1,0:T(2,128)} %pad_add_fusion.refs_0_, f32[4,100,256]{2,1,0:T(8,128)} %copy-done.7, f32[4,100,256]{2,1,0:T(8,128)} %copy-done.28, f32[100,2048]{1,0:T(8,128)} %get-tuple-element.86.refs_3_, ...), custom_call_target="tpu_custom_call" | custom-call | flops 17600000000 | bytes 1024 | tf_op jit(solution)/shard_map/pallas_call | solution.py:69
  365.1 12.5 %shard_map.308 = (bf16[400,2048]{1,0:T(8,128)(2,1)}, bf16[400,2048]{1,0:T(8,128)(2,1)}, f32[400,896]{1,0:T(8,128)}) custom-call(s32[1]{0:T(128)} %bitcast.18.refs_0_, f32[800,2048]{1,0:T(8,128)} %get-tuple-element.90.refs_1_, f32[800,2048]{1,0:T(8,128)} %all-gather.2.cloned.1.call-done.refs_0_.refs_9_.refs_2_, f32[2,6,400]{2,1,0:T(8,128)} %maximum_bitcast_fusion.refs_3_, ...), custom_call_target="tpu_custom_call" | custom-call | flops 9900000256 | bytes 1024 | tf_op jit(solution)/shard_map/pallas_call | solution.py:69
  379.6 17.0 %collective-permute-done.47.refs_1_ = f32[400,896]{1,0:T(8,128)S(1)} collective-permute-done((f32[400,896]{1,0:T(8,128)}, f32[400,896]{1,0:T(8,128)S(1)}, u32[]{:S(2)}, u32[]{:S(2)}) %collective-permute-start.47) | collective-permute-done | bytes 1433632 | tf_op jit(solution)/shard_map/ppermute | solution.py:630
  400.5 12.8 %shard_map.309 = (bf16[400,2048]{1,0:T(8,128)(2,1)}, bf16[400,2048]{1,0:T(8,128)(2,1)}, f32[400,896]{1,0:T(8,128)}) custom-call(s32[1]{0:T(128)} %bitcast.26.refs_0_, f32[800,2048]{1,0:T(8,128)} %get-tuple-element.90.refs_1_, f32[800,2048]{1,0:T(8,128)} %all-gather.2.cloned.1.call-done.refs_0_.refs_9_.refs_2_, f32[2,6,400]{2,1,0:T(8,128)} %maximum_bitcast_fusion.refs_3_, ...), custom_call_target="tpu_custom_call" | custom-call | flops 9900000256 | bytes 1024 | tf_op jit(solution)/shard_map/pallas_call | solution.py:69
  418.2 19.2 %shard_map.310.refs_2_ = f32[896,2048]{1,0:T(8,128)} custom-call(s32[1]{0:T(128)} %bitcast.18.refs_0_, bf16[896,800]{1,0:T(8,128)(2,1)} %get-tuple-element.82.refs_1_, bf16[896,800]{1,0:T(8,128)(2,1)} %get-tuple-element.83.refs_2_, bf16[400,2048]{1,0:T(8,128)(2,1)} %get-tuple-element.97.refs_3_, bf16[400,2048]{1,0:T(8,128)(2,1)} %get-tuple-element.98.refs_4_, ...), custom_call_target="tpu_custom_call" | custom-call | flops 19800000512 | bytes 1024 | tf_op jit(solution)/shard_map/pallas_call | solution.py:69
  437.4 13.6 %collective-permute-done.39.refs_1_ = f32[400,896]{1,0:T(8,128)S(1)} collective-permute-done((f32[400,896]{1,0:T(8,128)}, f32[400,896]{1,0:T(8,128)S(1)}, u32[]{:S(2)}, u32[]{:S(2)}) %collective-permute-start.39) | collective-permute-done | bytes 1433632 | tf_op jit(solution)/shard_map/ppermute | solution.py:630
  465.5 4.6 collective-permute-done.45
  (250 shorter events, 155.6 us)
Async XLA Ops:
  7.2 308.2 %all-gather.2.cloned.1.call-start = ((), (), s32[]{:S(2)}) async-start(), calls=%async_computation | async-start | bytes 7372800 | tf_op jit(solution)/shard_map/all_gather | solution.py:828
  14.6 22.2 %collective-permute-start.1 = (f32[800,256]{1,0:T(8,128)}, f32[800,256]{1,0:T(8,128)S(1)}, u32[]{:S(2)}, u32[]{:S(2)}) collective-permute-start(f32[800,256]{1,0:T(8,128)} %get-tuple-element.68), channel_id=1, source_target_pairs={{0,1},{1,0},{2,3},{3,2},{4,5},{5,4},{6,7},{7,6},{8,9},{9,8},{10,11... | collective-permute-start | bytes 2457608 | tf_op jit(solution)/shard_map/ppermute | solution.py:630
  25.6 31.8 %collective-permute-start.2 = (f32[800,256]{1,0:T(8,128)}, f32[800,256]{1,0:T(8,128)S(1)}, u32[]{:S(2)}, u32[]{:S(2)}) collective-permute-start(f32[800,256]{1,0:T(8,128)} %get-tuple-element.70), channel_id=1, source_target_pairs={{0,1},{1,0},{2,3},{3,2},{4,5},{5,4},{6,7},{7,6},{8,9},{9,8},{10,11... | collective-permute-start | bytes 2457608 | tf_op jit(solution)/shard_map/ppermute | solution.py:630
  38.1 19.5 %collective-permute-start.3 = (f32[800,256]{1,0:T(8,128)S(1)}, f32[800,256]{1,0:T(8,128)S(1)}, u32[]{:S(2)}, u32[]{:S(2)}) collective-permute-start(f32[800,256]{1,0:T(8,128)S(1)} %add.388), channel_id=1, source_target_pairs={{0,2},{1,3},{6,4},{7,5},{8,10},{9,11},{14,12},{15,13},{16,18},{17,... | collective-permute-start | bytes 2457608 | tf_op jit(solution)/shard_map/ppermute | solution.py:717
  55.8 21.5 %collective-permute-start.5 = (f32[800,256]{1,0:T(8,128)}, f32[800,256]{1,0:T(8,128)}, u32[]{:S(2)}, u32[]{:S(2)}) collective-permute-start(f32[800,256]{1,0:T(8,128)} %get-tuple-element.72), channel_id=1, source_target_pairs={{0,1},{1,0},{2,3},{3,2},{4,5},{5,4},{6,7},{7,6},{8,9},{9,8},{10,11... | collective-permute-start | bytes 2457608 | tf_op jit(solution)/shard_map/ppermute | solution.py:630
  60.1 17.2 %collective-permute-start.4 = (f32[800,256]{1,0:T(8,128)}, f32[800,256]{1,0:T(8,128)S(1)}, u32[]{:S(2)}, u32[]{:S(2)}) collective-permute-start(f32[800,256]{1,0:T(8,128)} %get-tuple-element.117), channel_id=1, source_target_pairs={{2,4},{3,5},{4,2},{5,3},{10,12},{11,13},{12,10},{13,11},{18,20},{1... | collective-permute-start | bytes 2457608 | tf_op jit(solution)/shard_map/ppermute | solution.py:719
  60.8 21.8 %collective-permute-start.7 = (f32[800,256]{1,0:T(8,128)}, f32[800,256]{1,0:T(8,128)}, u32[]{:S(2)}, u32[]{:S(2)}) collective-permute-start(f32[800,256]{1,0:T(8,128)} %get-tuple-element.118), channel_id=1, source_target_pairs={{0,2},{1,3},{6,4},{7,5},{8,10},{9,11},{14,12},{15,13},{16,18},{17,... | collective-permute-start | bytes 2457608 | tf_op jit(solution)/shard_map/ppermute | solution.py:718
  68.9 22.4 %collective-permute-start = (f32[800,256]{1,0:T(8,128)}, f32[800,256]{1,0:T(8,128)S(1)}, u32[]{:S(2)}, u32[]{:S(2)}) collective-permute-start(f32[800,256]{1,0:T(8,128)} %get-tuple-element.67), channel_id=1, source_target_pairs={{0,1},{1,0},{2,3},{3,2},{4,5},{5,4},{6,7},{7,6},{8,9},{9,8},{10,11... | collective-permute-start | bytes 2457608 | tf_op jit(solution)/shard_map/ppermute | solution.py:630
  84.3 16.6 %collective-permute-start.6 = (f32[800,256]{1,0:T(8,128)S(1)}, f32[800,256]{1,0:T(8,128)S(1)}, u32[]{:S(2)}, u32[]{:S(2)}) collective-permute-start(f32[800,256]{1,0:T(8,128)S(1)} %get-tuple-element.120), channel_id=1, source_target_pairs={{0,2},{1,3},{2,0},{3,1},{4,6},{5,7},{6,4},{7,5},{8,10},{9,11},{10,... | collective-permute-start | bytes 2457608 | tf_op jit(solution)/shard_map/ppermute | solution.py:720
  86.9 14.1 %collective-permute-start.8 = (f32[800,256]{1,0:T(8,128)S(1)}, f32[800,256]{1,0:T(8,128)S(1)}, u32[]{:S(2)}, u32[]{:S(2)}) collective-permute-start(f32[800,256]{1,0:T(8,128)S(1)} %get-tuple-element.119), channel_id=1, source_target_pairs={{2,4},{3,5},{4,2},{5,3},{10,12},{11,13},{12,10},{13,11},{18,20},{1... | collective-permute-start | bytes 2457608 | tf_op jit(solution)/shard_map/ppermute | solution.py:721
  139.2 16.1 %collective-permute-start.20 = (f32[4,100,256]{2,1,0:T(8,128)S(1)}, f32[4,100,256]{2,1,0:T(8,128)S(1)}, u32[]{:S(2)}, u32[]{:S(2)}) collective-permute-start(f32[4,100,256]{2,1,0:T(8,128)S(1)} %pad_maximum_fusion.refs_2_), channel_id=1, source_target_pairs={{0,1},{1,0},{2,3},{3,2},{4,5},{5,4},{6,7},{7,6},{8,9},{9,8},{10,11... | collective-permute-start | bytes 1228808 | tf_op jit(solution)/shard_map/ppermute | solution.py:630
  244.2 115.2 %collective-permute-start.46 = (f32[400,896]{1,0:T(8,128)}, f32[400,896]{1,0:T(8,128)S(1)}, u32[]{:S(2)}, u32[]{:S(2)}) collective-permute-start(f32[400,896]{1,0:T(8,128)} %shard_map.315), channel_id=1, source_target_pairs={{0,8},{8,0},{16,24},{24,16},{1,9},{9,1},{17,25},{25,17},{2,10},{10... | collective-permute-start | bytes 4300808 | tf_op jit(solution)/shard_map/ppermute | solution.py:630
  244.3 25.2 %collective-permute-start.31 = (f32[2,800]{1,0:T(2,128)S(1)}, f32[2,800]{1,0:T(2,128)S(1)}, u32[]{:S(2)}, u32[]{:S(2)}) collective-permute-start(f32[2,800]{1,0:T(2,128)S(1)} %copy-done.16), channel_id=1, source_target_pairs={{0,8},{8,0},{16,24},{24,16},{1,9},{9,1},{17,25},{25,17},{2,10},{10... | collective-permute-start | bytes 19208 | tf_op jit(solution)/shard_map/ppermute | solution.py:630
  270.7 39.0 %collective-permute-start.41 = (f32[4,100,100]{2,1,0:T(8,128)S(1)}, f32[4,100,100]{2,1,0:T(8,128)}, u32[]{:S(2)}, u32[]{:S(2)}) collective-permute-start(f32[4,100,100]{2,1,0:T(8,128)S(1)} %slice_select_fusion), channel_id=1, source_target_pairs={{0,4},{1,5},{2,6},{3,7},{4,0},{5,1},{6,2},{7,3},{8,12},{9,13},{10,... | collective-permute-start | bytes 480008 | tf_op jit(solution)/shard_map/ppermute | solution.py:630
  273.6 20.7 %collective-permute-start.23 = (f32[100,1024]{1,0:T(8,128)}, f32[100,1024]{1,0:T(8,128)S(1)}, u32[]{:S(2)}, u32[]{:S(2)}) collective-permute-start(f32[100,1024]{1,0:T(8,128)} %slice.165), channel_id=1, source_target_pairs={{0,1},{1,0},{2,3},{3,2},{4,5},{5,4},{6,7},{7,6},{8,9},{9,8},{10,11... | collective-permute-start | bytes 1228808 | tf_op jit(solution)/shard_map/ppermute | solution.py:630
  276.1 9.8 %collective-permute-start.33 = (f32[2,800]{1,0:T(2,128)S(1)}, f32[2,800]{1,0:T(2,128)S(1)}, u32[]{:S(2)}, u32[]{:S(2)}) collective-permute-start(f32[2,800]{1,0:T(2,128)S(1)} %add.426), channel_id=1, source_target_pairs={{0,1},{1,0},{2,3},{3,2},{4,5},{5,4},{6,7},{7,6},{8,9},{9,8},{10,11... | collective-permute-start | bytes 19208 | tf_op jit(solution)/shard_map/ppermute | solution.py:630
  314.9 17.8 %collective-permute-start.30 = (f32[4,100,256]{2,1,0:T(8,128)S(1)}, f32[4,100,256]{2,1,0:T(8,128)S(1)}, u32[]{:S(2)}, u32[]{:S(2)}) collective-permute-start(f32[4,100,256]{2,1,0:T(8,128)S(1)} %pad_maximum_fusion.1.refs_1_), channel_id=1, source_target_pairs={{0,1},{1,0},{2,3},{3,2},{4,5},{5,4},{6,7},{7,6},{8,9},{9,8},{10,11... | collective-permute-start | bytes 1228808 | tf_op jit(solution)/shard_map/ppermute | solution.py:630
  356.9 20.9 %collective-permute-start.42 = (f32[2,100,100]{2,1,0:T(8,128)S(1)}, f32[2,100,100]{2,1,0:T(8,128)S(1)}, u32[]{:S(2)}, u32[]{:S(2)}) collective-permute-start(f32[2,100,100]{2,1,0:T(8,128)S(1)} %slice_select_fusion.1), channel_id=1, source_target_pairs={{0,2},{1,3},{2,0},{3,1},{4,6},{5,7},{6,4},{7,5},{8,10},{9,11},{10,... | collective-permute-start | bytes 240008 | tf_op jit(solution)/shard_map/ppermute | solution.py:630
  363.3 33.4 %collective-permute-start.47 = (f32[400,896]{1,0:T(8,128)}, f32[400,896]{1,0:T(8,128)S(1)}, u32[]{:S(2)}, u32[]{:S(2)}) collective-permute-start(f32[400,896]{1,0:T(8,128)} %shard_map.316.refs_0_), channel_id=1, source_target_pairs={{0,16},{8,24},{16,0},{24,8},{1,17},{9,25},{17,1},{25,9},{2,18},{10... | collective-permute-start | bytes 4300808 | tf_op jit(solution)/shard_map/ppermute | solution.py:630
  377.7 35.6 %collective-permute-start.38 = (f32[400,896]{1,0:T(8,128)}, f32[400,896]{1,0:T(8,128)S(1)}, u32[]{:S(2)}, u32[]{:S(2)}) collective-permute-start(f32[400,896]{1,0:T(8,128)} %get-tuple-element.99.refs_7_), channel_id=1, source_target_pairs={{0,8},{8,0},{16,24},{24,16},{1,9},{9,1},{17,25},{25,17},{2,10},{10... | collective-permute-start | bytes 4300808 | tf_op jit(solution)/shard_map/ppermute | solution.py:630
  377.8 77.6 %collective-permute-start.43 = (f32[1,100,100]{2,1,0:T(8,128)S(1)}, f32[1,100,100]{2,1,0:T(8,128)S(1)}, u32[]{:S(2)}, u32[]{:S(2)}) collective-permute-start(f32[1,100,100]{2,1,0:T(8,128)S(1)} %slice_select_fusion.2), channel_id=1, source_target_pairs={{0,1},{1,0},{2,3},{3,2},{4,5},{5,4},{6,7},{7,6},{8,9},{9,8},{10,11... | collective-permute-start | bytes 120008 | tf_op jit(solution)/shard_map/ppermute | solution.py:630
  400.5 56.6 %collective-permute-start.48 = (f32[400,896]{1,0:T(8,128)}, f32[400,896]{1,0:T(8,128)S(1)}, u32[]{:S(2)}, u32[]{:S(2)}) collective-permute-start(f32[400,896]{1,0:T(8,128)} %shard_map.317.refs_1_), channel_id=1, source_target_pairs={{0,8},{8,0},{16,24},{24,16},{1,9},{9,1},{17,25},{25,17},{2,10},{10... | collective-permute-start | bytes 4300808 | tf_op jit(solution)/shard_map/ppermute | solution.py:630
  417.1 34.0 %collective-permute-start.39 = (f32[400,896]{1,0:T(8,128)}, f32[400,896]{1,0:T(8,128)S(1)}, u32[]{:S(2)}, u32[]{:S(2)}) collective-permute-start(f32[400,896]{1,0:T(8,128)} %shard_map.311.refs_0_), channel_id=1, source_target_pairs={{0,16},{8,24},{16,0},{24,8},{1,17},{9,25},{17,1},{25,9},{2,18},{10... | collective-permute-start | bytes 4300808 | tf_op jit(solution)/shard_map/ppermute | solution.py:630
  454.8 16.7 %collective-permute-start.40 = (f32[400,896]{1,0:T(8,128)}, f32[400,896]{1,0:T(8,128)S(1)}, u32[]{:S(2)}, u32[]{:S(2)}) collective-permute-start(f32[400,896]{1,0:T(8,128)} %shard_map.312.refs_1_), channel_id=1, source_target_pairs={{0,8},{8,0},{16,24},{24,16},{1,9},{9,1},{17,25},{25,17},{2,10},{10... | collective-permute-start | bytes 4300808 | tf_op jit(solution)/shard_map/ppermute | solution.py:630
  (56 other events, 442.5 us)
Sparse Core Ops, SparseCore 0:
  133.7 106.9 all-gather.1
